TPU v7x, 256 devices: a whole 4x4x8 slice. The times are simulated.
256 devices in a mesh: heads: 4 (over x_lo, core), blk: 64 (over x_hi, y, z).
Axes of the slice: x: 4 (x_hi: 2, x_lo: 2; x = x_hi * 2 + x_lo), y: 4, z: 8, core: 2. Of those that a mesh axis runs over, the one named last changes fastest.
Arguments:
- queries: bfloat16 [512, 128, 576], P('blk', 'heads'), may hold values from -12 to 12
- prefix_latent: bfloat16 [16384, 576], P('blk'), may hold values from -6 to 6
- suffix_latent: bfloat16 [512, 64, 576], P('blk'), may hold values from -10 to 10
- suffix_len: int32 [512], P('blk'), may hold values from 1 to 64, 16384 in all
- prefix_blocks: int32 [64], replicated, may hold values from 0 to 63, as said below
- caption_reach: int32 [512], P('blk'), may hold values from 1 to 64, as said below
- w_uv: bfloat16 [128, 512, 128], P('heads'), may hold values from -0.25 to 0.25
- w_out: bfloat16 [16384, 5120], P('heads', 'blk'), may hold values from -0.046875 to 0.046875
Outputs:
- mixed: bfloat16 [512, 5120], P('heads', 'blk')
Inputs may be any that keep to these rules, and one draw needn't show every extreme that they name: `suffix_len`: some caption has exactly 64 live suffix tokens. `prefix_blocks`: each of 0 to 63 once. `caption_reach`: some caption sees all 64 blocks and some only block 0.
All inputs are finite; a program needn't handle non-finite values. No bound on the sum of `suffix_len` on one device may be relied on, other than what follows from the above.
Results may differ from a plain program's by a relative error of at most 0.02.
Values may be sent and summed in bfloat16 or wider, within the bound.
A program may use at most 128 MiB of HBM per device.

v0:
```python
import jax
import jax.numpy as jnp
from jax import lax
from jax.sharding import PartitionSpec as P

SCALE = 192.0 ** (-0.5)
NEG = -1e30


def attend_rows(state, queries, rows, seen, width):
    best, total, summed = state
    scores = jnp.einsum("chd,rd->chr", queries, rows, preferred_element_type=jnp.float32) * SCALE
    mask = seen[:, None, :]
    scores = jnp.where(mask, scores, NEG)
    fresh = jnp.maximum(best, jnp.max(scores, axis=2))
    weights = jnp.where(mask, jnp.exp(scores - fresh[..., None]), jnp.float32(0.0))
    shrink = jnp.exp(best - fresh)
    total = total * shrink + jnp.sum(weights, axis=2)
    summed = summed * shrink[..., None] + jnp.einsum(
        "chr,rd->chd",
        weights.astype(jnp.bfloat16),
        rows[:, :width],
        preferred_element_type=jnp.float32,
    )
    return (fresh, total, summed)


def fold_rows(state, queries, piece, shard_rows, prefix_blocks, caption_reach, width):
    count = piece.shape[0]
    owner = jnp.arange(count, dtype=jnp.int32) // shard_rows
    numbers = jnp.arange(prefix_blocks.shape[0], dtype=jnp.int32)
    ident = jnp.sum(
        jnp.where(owner[:, None] == numbers[None, :], prefix_blocks[None, :], 0), axis=1
    )
    seen_all = ident[None, :] < caption_reach[:, None]
    factor = 1
    while factor * 2 * shard_rows <= 1024 and count % (factor * 2 * shard_rows) == 0:
        factor = factor * 2
    step_rows = factor * shard_rows
    steps = count // step_rows
    rows = piece.reshape(steps, step_rows, piece.shape[1])
    seen = jnp.transpose(seen_all.reshape(seen_all.shape[0], steps, step_rows), (1, 0, 2))

    def advance(carry, item):
        return (attend_rows(carry, queries, item[0], item[1], width), None)

    result, unused = lax.scan(advance, state, (rows, seen))
    return result


def suffix_state(queries, suffix_latent, suffix_len, width):
    scores = (
        jnp.einsum("chd,csd->chs", queries, suffix_latent, preferred_element_type=jnp.float32)
        * SCALE
    )
    positions = jnp.arange(suffix_latent.shape[1], dtype=jnp.int32)
    live = (positions[None, :] < suffix_len[:, None])[:, None, :]
    scores = jnp.where(live, scores, NEG)
    best = jnp.max(scores, axis=2)
    weights = jnp.where(live, jnp.exp(scores - best[..., None]), jnp.float32(0.0))
    total = jnp.sum(weights, axis=2)
    summed = jnp.einsum(
        "chs,csd->chd",
        weights.astype(jnp.bfloat16),
        suffix_latent[:, :, :width],
        preferred_element_type=jnp.float32,
    )
    return (best, total, summed)


def per_device(
    queries, prefix_latent, suffix_latent, suffix_len, prefix_blocks, caption_reach, w_uv, w_out
):
    width = w_uv.shape[1]
    shard_rows = prefix_latent.shape[0]
    captions = queries.shape[0]
    local_heads = queries.shape[1]
    own = suffix_state(queries, suffix_latent, suffix_len, width)
    top, total, summed = fold_rows(
        own,
        queries,
        lax.all_gather(prefix_latent, "blk", axis=0, tiled=True),
        shard_rows,
        prefix_blocks,
        caption_reach,
        width,
    )
    attn = (summed / total[..., None]).astype(jnp.bfloat16)
    head_value = jnp.einsum("chl,hlv->chv", attn, w_uv, preferred_element_type=jnp.float32).astype(
        jnp.bfloat16
    )
    flat = head_value.reshape(captions, local_heads * w_uv.shape[2])
    partial_sums = jnp.dot(
        lax.all_gather(flat, "blk", axis=0, tiled=True), w_out, preferred_element_type=jnp.float32
    )
    return lax.psum_scatter(
        partial_sums.astype(jnp.bfloat16), "heads", scatter_dimension=0, tiled=True
    )


def solution(mesh):
    placed = (
        P("blk", "heads", None),
        P("blk", None),
        P("blk", None, None),
        P("blk"),
        P(),
        P("blk"),
        P("heads", None, None),
        P("heads", "blk"),
    )
    return jax.shard_map(
        per_device, mesh=mesh, in_specs=placed, out_specs=P("heads", "blk"), check_vma=False
    )
```

profile of v0, /device:TPU:2, one launch (start us, length us, event | category | flops | bytes accessed | tf_op | source)
XLA Modules:
  0.0 485.3 jit_solution(6745721646079804347)
XLA Ops:
  7.3 1.4 select_reduce_fusion
  9.5 1.6 fusion.28
  13.4 228.8 %all-gather.3.cloned.1.call-done = bf16[16384,576]{0,1:T(8,128)(2,1)} async-done(((bf16[256,576]{0,1:T(8,128)(2,1)}), bf16[16384,576]{0,1:T(8,128)(2,1)}) %all-gather.3.cloned.1.call-update) | async-done | bytes 18874384 | tf_op jit(solution)/shard_map/all_gather | solution.py:82
  242.2 16.9 %copy.28 = bf16[72,16,8,1024]{3,2,0,1:T(8,128)(2,1)} copy(bf16[72,16,8,1024]{3,2,1,0:T(8,128)(2,1)} %bitcast.42) | data formatting | bytes 37748736 | tf_op jit(solution)/shard_map/reshape | solution.py:41
  259.1 69.5 %while.14 = (s32[]{:T(128)}, f32[8,32]{1,0:T(8,128)S(1)}, f32[8,32]{1,0:T(8,128)S(1)}, f32[8,32,512]{2,1,0:T(8,128)S(1)}, pred[16,8,1024]{2,1,0:T(8,128)(4,1)S(1...) while((s32[]{:T(128)}, f32[8,32]{1,0:T(8,128)S(1)}, ...), condition=%wide.region_6.7_spmd, body=%wide.region_3.6_spmd.sunk | while | flops 573047296 | bytes 9140329 | solution.py:47
  259.1 1.9 fusion.41
  261.5 1.4 dynamic-slice_bitcast_fusion.5
  263.4 1.9 fusion.41
  265.8 1.4 dynamic-slice_bitcast_fusion.5
  267.8 1.9 fusion.41
  270.2 1.4 dynamic-slice_bitcast_fusion.5
  272.1 1.9 fusion.41
  274.5 1.4 dynamic-slice_bitcast_fusion.5
  276.5 1.9 fusion.41
  278.8 1.4 dynamic-slice_bitcast_fusion.5
  280.8 1.9 fusion.41
  285.2 1.9 fusion.41
  289.5 1.9 fusion.41
  293.9 1.9 fusion.41
  298.2 1.9 fusion.41
  302.5 1.9 fusion.41
  304.9 1.4 dynamic-slice_bitcast_fusion.5
  306.9 1.9 fusion.41
  311.2 1.9 fusion.41
  315.6 1.9 fusion.41
  319.9 1.9 fusion.41
  324.2 1.9 fusion.41
  328.7 3.6 fusion.13
  332.3 125.0 %all-gather.5.cloned.1.call-done = bf16[512,4096]{1,0:T(8,128)(2,1)} async-done(((bf16[8,4096]{1,0:T(8,128)(2,1)}), bf16[512,4096]{1,0:T(8,128)(2,1)}) %all-gather.5.cloned.1.call-update) | async-done | bytes 4194320 | tf_op jit(solution)/shard_map/all_gather | solution.py:94
  457.3 3.6 convolution_convert_fusion
  461.7 15.6 %reduce-scatter.4.cloned.1.call-done = bf16[128,80]{1,0:T(8,128)(2,1)} async-done(((bf16[512,80]{1,0:T(8,128)(2,1)}), bf16[128,80]{1,0:T(8,128)(2,1)}) %reduce-scatter.4.cloned.1.call-update) | async-done | bytes 20496
  477.3 1.5 copy.23
  (124 shorter events, 34.1 us)
Async XLA Ops:
  6.5 450.8 %copy-start = (bf16[4096,80]{0,1:T(8,128)(2,1)S(1)}, bf16[4096,80]{0,1:T(8,128)(2,1)}, u32[]{:S(2)}) copy-start(bf16[4096,80]{0,1:T(8,128)(2,1)} %param.17) | copy-start | bytes 1966084
  6.5 235.7 %all-gather.3.cloned.1.call-start = ((), (), s32[]{:S(2)}) async-start(), calls=%async_computation.1 | async-start | bytes 19169280 | tf_op jit(solution)/shard_map/all_gather | solution.py:82
  7.3 450.1 %all-gather.5.cloned.1.call-start = ((), (), s32[]{:S(2)}) async-start(), calls=%async_computation.2 | async-start | bytes 4259840 | tf_op jit(solution)/shard_map/all_gather | solution.py:94
  242.2 16.9 %copy-start.1 = (bf16[8,32,576]{2,1,0:T(8,128)(2,1)S(1)}, bf16[8,32,576]{2,1,0:T(8,128)(2,1)}, u32[]{:S(2)}) copy-start(bf16[8,32,576]{2,1,0:T(8,128)(2,1)} %param.10) | copy-start | bytes 884740
  332.3 145.0 %reduce-scatter.4.cloned.1.call-start = ((), (), s32[]{:S(2)}) async-start(), calls=%async_computation.3 | async-start | bytes 163840
Sparse Core Ops, SparseCore 0:
  10.8 231.3 all-gather.2
  332.4 124.8 all-gather.4
  461.8 15.4 reduce-scatter.3
where the time goes:
time: 489 us; the launch traced here: 485 us
  waiting for transfers between devices  370 us (76%)
  matrix products  50.5 us (10%)
  local copies, waits for them, and re-layouts  41 us (8%)
  between operations  13.2 us (3%)
  other arithmetic  9.51 us (2%)
    all_gather x1, waiting for transfers between devices, per_device(): lax.all_gather(prefix_latent, 'blk', axis=0, tiled=True)  229 us
    all_gather x1, waiting for transfers between devices, per_device(): lax.all_gather(flat, 'blk', axis=0, tiled=True)  125 us
    dot_general x16, matrix products, attend_rows(): jnp.einsum('chd,rd->chr', queries, rows, preferred_element_type=jnp.float32)  31.1 us
    squeeze x16, local copies, waits for them, and re-layouts, fold_rows(): result, unused = lax.scan(advance, state, (rows, seen))  21.7 us
    reshape x1, local copies, waits for them, and re-layouts, fold_rows(): rows = piece.reshape(steps, step_rows, piece.shape[1])  16.9 us
    unnamed x4, waiting for transfers between devices  16.3 us
  transfers between devices with their start and end apart: 3, of which 3 were waited for; matrix products, arithmetic and copies ran while one was open for 1% of the time, Pallas kernels for 0%

commit v1 on v0

v1 whole, which is shorter than its diff:
```python
import jax
import jax.numpy as jnp
from jax import lax
from jax.experimental import pallas as pl
from jax.experimental.pallas import tpu as pltpu
from jax.sharding import PartitionSpec as P

C2 = (192.0 ** -0.5) * 1.4426950408889634
NEG = -1.0e30
NT = (((1,), (1,)), ((), ()))
NN = (((1,), (0,)), ((), ()))
F32 = jnp.float32
BF16 = jnp.bfloat16
MESH = pl.DeviceIdType.MESH


def dot(a, b, dims):
    return lax.dot_general(a, b, dims, preferred_element_type=F32)


def kernel(
    q_hbm, k_hbm, s_hbm, uv_hbm, w_hbm, len_ref, blocks_ref, reach_ref, out_ref,
    q_in, k_in, s_in, uv, w_in,
    qbuf, kbuf, acc, m_ref, l_ref,
    w_t, wbuf, hv_send, lse_full, lse_send, hv_recv, lse_recv,
    units, hv_all, out_send, rs,
    in_sem, kz_s, kz_r, kx_s, kx_r, kc_s, kc_r, q_s, q_r, w_s, w_r,
    a_s, a_r, h_s, h_r, rs_s, rs_r,
):
    hd = lax.axis_index("heads")
    b = lax.axis_index("blk")
    p, c = hd // 2, hd % 2
    xh, y, z = b // 32, (b // 8) % 4, b % 8

    def dev(xh_=None, y_=None, z_=None, p_=None, c_=None):
        xx = xh if xh_ is None else xh_
        yy = y if y_ is None else y_
        zz = z if z_ is None else z_
        pp = p if p_ is None else p_
        cc = c if c_ is None else c_
        return (pp * 2 + cc, xx * 32 + yy * 8 + zz)

    zp, zm = dev(z_=(z + 1) % 8), dev(z_=(z + 7) % 8)
    same_x, other_x = dev(p_=1 - p), dev(xh_=1 - xh, p_=1 - p)
    sib, across = dev(c_=1 - c), dev(xh_=1 - xh)

    def peer(d, dh):
        return dev(
            y_=(y + 4 - d) % 4,
            p_=p if dh // 2 == 0 else 1 - p,
            c_=c if dh % 2 == 0 else 1 - c,
        )

    local = []
    for n, (src, dst) in enumerate(
        ((q_hbm, q_in), (k_hbm, k_in), (s_hbm, s_in), (w_hbm, w_in), (uv_hbm, uv))
    ):
        copy = pltpu.make_async_copy(src, dst, in_sem.at[n])
        copy.start()
        local.append(copy)

    partners = [zp, zm, other_x, across]
    partners += [peer(d, dh) for d in range(4) for dh in range(4) if d or dh]
    barrier = pltpu.get_barrier_semaphore()
    for who in partners:
        pl.semaphore_signal(barrier, inc=1, device_id=who, device_id_type=MESH)

    sent = []

    def send(src, dst, ssem, rsem, who):
        copy = pltpu.make_async_remote_copy(
            src_ref=src, dst_ref=dst, send_sem=ssem, recv_sem=rsem,
            device_id=who, device_id_type=MESH,
        )
        copy.start()
        sent.append(copy)
        return copy

    lanes = lax.broadcasted_iota(jnp.int32, (1, 64), 1)
    local[1].wait()
    own = (lanes == blocks_ref[b]).astype(F32)
    kbuf[0, 0:256, 0:576] = k_in[...]
    kbuf[0, 0:256, 576:640] = jnp.broadcast_to(own, (256, 64)).astype(BF16)
    local[0].wait()
    qbuf[0, :, 0:576] = q_in[...]
    for i in range(8):
        seen = jnp.where(lanes >= reach_ref[i], F32(NEG), F32(0.0))
        qbuf[0, 32 * i : 32 * i + 32, 576:640] = jnp.broadcast_to(seen, (32, 64)).astype(BF16)

    pl.semaphore_wait(barrier, len(partners))

    quarter = pl.ds(pl.multiple_of(128 * p + 64 * c, 64), 64)
    quarter_x = pl.ds(pl.multiple_of(128 * (1 - p) + 64 * c, 64), 64)
    ox = [
        send(kbuf.at[0, quarter_x], kbuf.at[0, 256:320], kx_s.at[0, 0], kx_r.at[0, 0], other_x)
    ]
    kz = {}

    def ring(buf, r, xb, src, dst, s_sem, r_sem, table):
        forward = r <= 3 or (r == 4 and xb == 0)
        table[r, xb] = send(src, dst, s_sem.at[r, xb], r_sem.at[r, xb], zp if forward else zm)

    def k_rows(r, xb):
        return kbuf.at[r, 64 * xb : 64 * xb + 64]

    for r in (1, 7):
        ring(kbuf, r, 0, kbuf.at[0, quarter], k_rows(r, 0), kz_s, kz_r, kz)
    qp = send(qbuf.at[0], qbuf.at[1], q_s.at[0], q_r.at[0], dev(y_=(y + 1) % 4))
    qm = send(qbuf.at[0], qbuf.at[3], q_s.at[1], q_r.at[1], dev(y_=(y + 3) % 4))
    ox.append(
        send(kbuf.at[0, quarter], kbuf.at[0, 320:384], kx_s.at[0, 1], kx_r.at[0, 1], other_x)
    )
    local[2].wait()
    m_ref[...] = jnp.full_like(m_ref, NEG)
    l_ref[...] = jnp.zeros_like(l_ref)
    acc[...] = jnp.zeros_like(acc)
    ox[0].wait_recv()
    for r in (1, 7):
        ring(kbuf, r, 1, kbuf.at[0, 256:320], k_rows(r, 1), kz_s, kz_r, kz)

    spot = lax.broadcasted_iota(jnp.int32, (1, 64), 1)

    def suffix(i, carry):
        rows = pl.ds(pl.multiple_of(i * 32, 32), 32)
        toks = pl.ds(pl.multiple_of(i * 64, 64), 64)
        sc = dot(qbuf[0, rows, 0:576], s_in[toks, :], NT) * C2
        sc = jnp.where(spot < len_ref[i], sc, F32(NEG))
        top = jnp.max(sc, axis=1, keepdims=True)
        weight = jnp.exp2(sc - top)
        m_ref[rows, :] = jnp.broadcast_to(top, (32, 128))
        l_ref[rows, :] = jnp.broadcast_to(jnp.sum(weight, axis=1, keepdims=True), (32, 128))
        start = dot(weight.astype(BF16), s_in[toks, 0:512], NN)
        for j in range(4):
            acc[j, rows, :] = start[:, 128 * j : 128 * j + 128]
        return carry

    lax.fori_loop(0, 8, suffix, 0)

    ox[1].wait_recv()
    sib0 = send(kbuf.at[0, 256:384], kbuf.at[0, 384:512], kc_s.at[0, 0], kc_r.at[0, 0], sib)

    def score(s, r):
        return dot(qbuf[s], kbuf[r], NT)

    def fold(s, r, sc):
        rows = pl.ds(s * 256, 256)
        before = m_ref[rows, :]
        after = jnp.maximum(before, jnp.max(sc, axis=1, keepdims=True) * C2)
        shrink = jnp.exp2(before - after)
        weight = jnp.exp2(sc * C2 - after[:, :1])
        l_ref[rows, :] = l_ref[rows, :] * shrink + jnp.sum(weight, axis=1, keepdims=True)
        m_ref[rows, :] = after
        more = dot(weight.astype(BF16), kbuf[r, :, 0:512], NN)
        for j in range(4):
            acc[j, rows, :] = acc[j, rows, :] * shrink + more[:, 128 * j : 128 * j + 128]

    def attend(todo):
        now = score(*todo[0])
        for n, (s, r) in enumerate(todo):
            later = score(*todo[n + 1]) if n + 1 < len(todo) else None
            fold(s, r, now)
            now = later

    kx, kc = {}, {}

    def from_z(r):
        for xb in (0, 1):
            kz[r, xb].wait_recv()
            if r in (1, 2):
                ring(kbuf, r + 1, xb, k_rows(r, xb), k_rows(r + 1, xb), kz_s, kz_r, kz)
            elif r in (7, 6):
                ring(kbuf, r - 1, xb, k_rows(r, xb), k_rows(r - 1, xb), kz_s, kz_r, kz)
            elif (r, xb) in ((3, 0), (5, 1)):
                ring(kbuf, 4, xb, k_rows(r, xb), k_rows(4, xb), kz_s, kz_r, kz)
            if xb == 0:
                kx[r] = (
                    send(kbuf.at[r, 0:64], kbuf.at[r, 128:192], kx_s.at[r, 0], kx_r.at[r, 0], same_x),
                    send(kbuf.at[r, 0:64], kbuf.at[r, 192:256], kx_s.at[r, 1], kx_r.at[r, 1], other_x),
                )
        kc[r] = [send(kbuf.at[r, 0:128], kbuf.at[r, 256:384], kc_s.at[r, 0], kc_r.at[r, 0], sib)]

    def from_x(r):
        for copy in kx[r]:
            copy.wait_recv()
        kc[r].append(
            send(kbuf.at[r, 128:256], kbuf.at[r, 384:512], kc_s.at[r, 1], kc_r.at[r, 1], sib)
        )

    def ready(r):
        for copy in kc[r]:
            copy.wait_recv()

    local[3].wait()

    def turn(i, carry):
        w_t[i] = w_in[pl.ds(pl.multiple_of(i * 1024, 1024), 1024), :].T
        return carry

    lax.fori_loop(0, 4, turn, 0)
    wbuf[0:80, :] = w_t[y]

    sib0.wait_recv()
    attend([(0, 0)])
    from_z(1)
    from_z(7)
    from_x(1)
    from_x(7)
    ready(1)
    ready(7)
    attend([(0, 1), (0, 7)])
    qp.wait_recv()
    qfp = send(qbuf.at[1, 0:128], qbuf.at[2, 0:128], q_s.at[2], q_r.at[2], dev(y_=(y + 1) % 4))
    qm.wait_recv()
    qfm = send(qbuf.at[3, 128:256], qbuf.at[2, 128:256], q_s.at[3], q_r.at[3], dev(y_=(y + 3) % 4))
    ws = [
        send(w_t.at[(y + d) % 4], wbuf.at[80 * d : 80 * d + 80], w_s.at[d], w_r.at[d], dev(y_=(y + d) % 4))
        for d in (1, 3, 2)
    ]
    from_z(2)
    from_z(6)
    attend([(1, 0), (3, 0), (1, 1), (3, 1)])
    from_x(2)
    from_x(6)
    attend([(1, 7), (3, 7)])
    ready(2)
    ready(6)
    from_z(3)
    from_z(5)
    attend([(0, 2), (1, 2), (3, 2)])
    from_x(3)
    from_x(5)
    from_z(4)
    attend([(0, 6), (1, 6), (3, 6)])
    qfp.wait_recv()
    qfm.wait_recv()
    from_x(4)
    attend([(2, 0), (2, 1), (2, 7), (2, 2), (2, 6)])
    ready(3)
    ready(5)
    ready(4)

    def last(i, carry):
        r = 3 + i
        attend([(0, r), (1, r), (2, r), (3, r)])
        return carry

    lax.fori_loop(0, 3, last, 0)

    local[4].wait()

    def up(h, carry):
        parts, logs = [], []
        for a in range(4):
            s = (y + 4 - a) % 4
            rows = pl.ds(s * 256 + h, 8, stride=32)
            tot = l_ref[rows, :]
            inv = 1.0 / tot
            parts.append(jnp.concatenate([acc[j, rows, :] * inv for j in range(4)], axis=1))
            logs.append(m_ref[rows, :] + jnp.log2(tot))
        attn = jnp.concatenate(parts, axis=0).astype(BF16)
        value = dot(attn, uv[h], NN)
        place = pl.ds(pl.multiple_of((h % 8) * 32, 32), 32)
        hv_send[h // 8, place, :] = value.astype(BF16)
        lse_full[h // 8, place, :] = jnp.concatenate(logs, axis=0)
        return carry

    lax.fori_loop(0, 32, up, 0)

    def flat(i, carry):
        lse_send[i] = lse_full[i].T[0:8, :]
        return carry

    lax.fori_loop(0, 4, flat, 0)

    heads_out = []
    for d in (2, 1, 3):
        to = (y + d) % 4
        heads_out.append(
            (
                send(hv_send.at[to], hv_recv.at[d], a_s.at[d, 0], a_r.at[d, 0], dev(y_=to)),
                send(lse_send.at[to], lse_recv.at[d], a_s.at[d, 1], a_r.at[d, 1], dev(y_=to)),
            )
        )
    for pair in heads_out:
        for copy in pair:
            copy.wait_recv()
    logs = [lse_send[y]] + [lse_recv[d] for d in (1, 2, 3)]
    best = jnp.maximum(jnp.maximum(logs[0], logs[1]), jnp.maximum(logs[2], logs[3]))
    part = [jnp.exp2(x - best) for x in logs]
    norm = 1.0 / (part[0] + part[1] + part[2] + part[3])
    total = None
    for d in range(4):
        share = jnp.concatenate([part[d] * norm] * 16, axis=0).T
        term = share * (hv_send[y] if d == 0 else hv_recv[d]).astype(F32)
        total = term if d == 0 else total + term
    total = total.astype(BF16)
    for h in range(8):
        units[0, 0, :, 128 * h : 128 * h + 128] = total[32 * h : 32 * h + 32, :]

    hz = {}
    hx = send(units.at[0, 0], units.at[0, 1], h_s.at[0, 0], h_r.at[0, 0], across)
    for r in (1, 7):
        ring(units, r, 0, units.at[0, 0], units.at[r, 0], h_s, h_r, hz)

    def place_unit(r, xb):
        base = (xh if xb == 0 else 1 - xh) * 256 + ((z + 8 - r) % 8) * 8
        unit = units[r, xb].astype(F32)
        for a in range(4):
            hv_all[pl.ds(pl.multiple_of(base + 64 * a, 8), 8), :] = unit[8 * a : 8 * a + 8, :]

    place_unit(0, 0)
    hx.wait_recv()
    for r in (1, 7):
        ring(units, r, 1, units.at[0, 1], units.at[r, 1], h_s, h_r, hz)
    place_unit(0, 1)
    for r in (1, 7, 2, 6, 3, 5, 4):
        for xb in (0, 1):
            hz[r, xb].wait_recv()
            if r in (1, 2):
                ring(units, r + 1, xb, units.at[r, xb], units.at[r + 1, xb], h_s, h_r, hz)
            elif r in (7, 6):
                ring(units, r - 1, xb, units.at[r, xb], units.at[r - 1, xb], h_s, h_r, hz)
            elif (r, xb) in ((3, 0), (5, 1)):
                ring(units, 4, xb, units.at[r, xb], units.at[4, xb], h_s, h_r, hz)
        for xb in (0, 1):
            place_unit(r, xb)

    for copy in ws:
        copy.wait_recv()
    for h in range(4):
        cols = dot(wbuf[...], hv_all[128 * h : 128 * h + 128, :].astype(BF16), NT)
        out_send[h] = cols.astype(BF16)
    back = []
    for d in (2, 1, 3, 0):
        for dh in range(4):
            if d or dh:
                who = peer(d, dh)
                back.append(
                    send(
                        out_send.at[who[0], 80 * d : 80 * d + 80], rs.at[4 * d + dh],
                        rs_s.at[4 * d + dh], rs_r.at[4 * d + dh], who,
                    )
                )
    result = out_send[hd, 0:80, :].astype(F32)
    for copy in back:
        copy.wait_recv()
    for n in range(1, 16):
        result = result + rs[n].astype(F32)
    out_ref[...] = result.T.astype(BF16)
    for copy in sent:
        copy.wait_send()


def per_device(
    queries, prefix_latent, suffix_latent, suffix_len, prefix_blocks, caption_reach, w_uv, w_out
):
    dma = pltpu.SemaphoreType.DMA
    return pl.pallas_call(
        kernel,
        out_shape=jax.ShapeDtypeStruct((128, 80), BF16),
        in_specs=[pl.BlockSpec(memory_space=pl.ANY)] * 5
        + [pl.BlockSpec(memory_space=pltpu.SMEM)] * 3,
        out_specs=pl.BlockSpec(memory_space=pltpu.VMEM),
        scratch_shapes=[
            pltpu.VMEM((256, 576), BF16),
            pltpu.VMEM((256, 576), BF16),
            pltpu.VMEM((512, 576), BF16),
            pltpu.VMEM((32, 512, 128), BF16),
            pltpu.VMEM((4096, 80), BF16),
            pltpu.VMEM((4, 256, 640), BF16),
            pltpu.VMEM((8, 512, 640), BF16),
            pltpu.VMEM((4, 1024, 128), F32),
            pltpu.VMEM((1024, 128), F32),
            pltpu.VMEM((1024, 128), F32),
            pltpu.VMEM((4, 80, 1024), BF16),
            pltpu.VMEM((320, 1024), BF16),
            pltpu.VMEM((4, 256, 128), BF16),
            pltpu.VMEM((4, 256, 128), F32),
            pltpu.VMEM((4, 8, 256), F32),
            pltpu.VMEM((4, 256, 128), BF16),
            pltpu.VMEM((4, 8, 256), F32),
            pltpu.VMEM((8, 2, 32, 1024), BF16),
            pltpu.VMEM((512, 1024), F32),
            pltpu.VMEM((4, 320, 128), BF16),
            pltpu.VMEM((16, 80, 128), BF16),
            dma((5,)),
            dma((8, 2)), dma((8, 2)),
            dma((8, 2)), dma((8, 2)),
            dma((8, 2)), dma((8, 2)),
            dma((4,)), dma((4,)),
            dma((4,)), dma((4,)),
            dma((4, 2)), dma((4, 2)),
            dma((8, 2)), dma((8, 2)),
            dma((16,)), dma((16,)),
        ],
        compiler_params=pltpu.CompilerParams(
            collective_id=0, has_side_effects=True, vmem_limit_bytes=56 * 2**20
        ),
    )(
        queries.reshape(256, 576),
        prefix_latent,
        suffix_latent.reshape(512, 576),
        w_uv,
        w_out,
        suffix_len,
        prefix_blocks,
        caption_reach,
    )


def solution(mesh):
    placed = (
        P("blk", "heads", None),
        P("blk", None),
        P("blk", None, None),
        P("blk"),
        P(),
        P("blk"),
        P("heads", None, None),
        P("heads", "blk"),
    )
    return jax.shard_map(
        per_device, mesh=mesh, in_specs=placed, out_specs=P("heads", "blk"), check_vma=False
    )
```

time: 489 us -> 98.6 us (0.20)
  waiting for transfers between devices: 370 us -> 0 us
  Pallas kernels: 0 us -> 91.7 us
  matrix products: 50.5 us -> 0 us
  local copies, waits for them, and re-layouts: 41 us -> 5.54 us
  between operations: 13.2 us -> 0.01 us
  other arithmetic: 9.51 us -> 0 us
    all_gather x2 -> x0, waiting for transfers between devices: 354 us -> none  [the longest x1 229 us: per_device(): lax.all_gather(prefix_latent, 'blk', axis=0, tiled=True)]
    pallas_call x0 -> x1, Pallas kernels: none -> 91.7 us  [per_device(): pl.pallas_call(kernel, out_shape=jax.ShapeDtypeStruct((128, 80), BF16), i...]
    dot_general x36 -> x0, matrix products: 50.5 us -> none  [the longest x16 31.1 us: attend_rows(): jnp.einsum('chd,rd->chr', queries, rows, preferred_element_type=jnp.float32)]
    squeeze x16 -> x0, local copies, waits for them, and re-layouts: 21.7 us -> none  [fold_rows(): result, unused = lax.scan(advance, state, (rows, seen))]
    reshape x1 -> x0, local copies, waits for them, and re-layouts: 16.9 us -> none  [fold_rows(): rows = piece.reshape(steps, step_rows, piece.shape[1])]
    unnamed x4 -> x0, waiting for transfers between devices: 16.3 us -> none
    reduce_sum x18 -> x0, other arithmetic: 7.64 us -> none  [the longest x16 6.05 us: attend_rows(): total = total * shrink + jnp.sum(weights, axis=2)]
  transfers between devices with their start and end apart: 3 -> 0, of which waited for: 3 -> 0; matrix products, arithmetic and copies ran while one was open for 1% -> 0% of each run, Pallas kernels for 0% -> 0%
where the time goes in v1:
time: 98.6 us; the launch traced here: 97.3 us
  Pallas kernels  91.7 us (93%)
  local copies, waits for them, and re-layouts  5.54 us (6%)
    pallas_call x1, Pallas kernels, per_device(): pl.pallas_call(kernel, out_shape=jax.ShapeDtypeStruct((128, 80), BF16), i...  91.7 us
    unnamed x2, local copies, waits for them, and re-layouts  4.09 us

profile of v1, /device:TPU:2, one launch (start us, length us, event | category | flops | bytes accessed | tf_op | source)
XLA Modules:
  0.0 97.3 jit_solution(5389297040613680755)
XLA Ops:
  0.0 1.9 %copy.9.k_hbm = bf16[256,576]{1,0:T(8,128)(2,1)} copy(bf16[256,576]{0,1:T(8,128)(2,1)} %param.9) | data formatting | bytes 589824 | tf_op args[1]
  1.9 2.2 %copy.10.w_hbm = bf16[4096,80]{1,0:T(8,128)(2,1)} copy(bf16[4096,80]{0,1:T(8,128)(2,1)} %param.15) | data formatting | bytes 1310720 | tf_op args[7]
  4.1 91.7 %shard_map.82 = bf16[128,80]{1,0:T(8,128)(2,1)} custom-call(bf16[256,576]{1,0:T(8,128)(2,1)} %bitcast.3, bf16[256,576]{1,0:T(8,128)(2,1)} %copy.9.k_hbm, bf16[512,576]{1,0:T(8,128)(2,1)} %bitcast.2, bf16[32,512,128]{2,1,0:T(8,128)(2,1)} %uv_hbm.1, bf16[4096,80]{1,0:T(8,128)(2,1)} %copy.10.w_hbm, s32[8]{0:T(128)} %len_ref.1, s32[64]{0:T(128)} %blocks_ref.1, ...), custom_call_target="tpu_custom_call" | custom-call | tf_op jit(solution)/shard_map/pallas_call | solution.py:358
  95.8 1.5 %copy.11 = bf16[128,80]{0,1:T(8,128)(2,1)} copy(bf16[128,80]{1,0:T(8,128)(2,1)} %shard_map.82) | data formatting | bytes 40960 | tf_op jit(solution)/shard_map/pallas_call | solution.py:358

commit v2 on v1

v2 whole, which is shorter than its diff:
```python
import jax
import jax.numpy as jnp
from jax import lax
from jax.experimental import pallas as pl
from jax.experimental.pallas import tpu as pltpu
from jax.sharding import PartitionSpec as P

C2 = (192.0 ** -0.5) * 1.4426950408889634
NEG = -1.0e30
NT = (((1,), (1,)), ((), ()))
NN = (((1,), (0,)), ((), ()))
F32 = jnp.float32
BF16 = jnp.bfloat16
MESH = pl.DeviceIdType.MESH


def dot(a, b, dims):
    return lax.dot_general(a, b, dims, preferred_element_type=F32)


def kernel(
    q_hbm, k_hbm, s_hbm, uv_hbm, w_hbm, len_ref, blocks_ref, reach_ref, out_ref,
    q_in, k_in, s_in, uv, w_in,
    qbuf, kbuf, acc, m_ref, l_ref,
    wbuf, hv_send, lse_full, lse_send, hv_recv, lse_recv,
    units, hv_all, out_send, rs,
    in_sem, kz_s, kz_r, kx_s, kx_r, kc_s, kc_r, q_s, q_r, w_s, w_r,
    a_s, a_r, h_s, h_r, rs_s, rs_r,
):
    hd = lax.axis_index("heads")
    b = lax.axis_index("blk")
    p, c = hd // 2, hd % 2
    xh, y, z = b // 32, (b // 8) % 4, b % 8

    def dev(xh_=None, y_=None, z_=None, p_=None, c_=None):
        xx = xh if xh_ is None else xh_
        yy = y if y_ is None else y_
        zz = z if z_ is None else z_
        pp = p if p_ is None else p_
        cc = c if c_ is None else c_
        return (pp * 2 + cc, xx * 32 + yy * 8 + zz)

    zp, zm = dev(z_=(z + 1) % 8), dev(z_=(z + 7) % 8)
    same_x, other_x = dev(p_=1 - p), dev(xh_=1 - xh, p_=1 - p)
    sib, across = dev(c_=1 - c), dev(xh_=1 - xh)

    def peer(d, dh):
        return dev(
            y_=(y + 4 - d) % 4,
            p_=p if dh // 2 == 0 else 1 - p,
            c_=c if dh % 2 == 0 else 1 - c,
        )

    local = []
    for n, (src, dst) in enumerate(
        ((q_hbm, q_in), (k_hbm, k_in), (s_hbm, s_in), (w_hbm, w_in), (uv_hbm, uv))
    ):
        copy = pltpu.make_async_copy(src, dst, in_sem.at[n])
        copy.start()
        local.append(copy)

    partners = [zp, zm, other_x, across]
    partners += [peer(d, dh) for d in range(4) for dh in range(4) if d or dh]
    barrier = pltpu.get_barrier_semaphore()
    for who in partners:
        pl.semaphore_signal(barrier, inc=1, device_id=who, device_id_type=MESH)

    sent = []

    def send(src, dst, ssem, rsem, who):
        copy = pltpu.make_async_remote_copy(
            src_ref=src, dst_ref=dst, send_sem=ssem, recv_sem=rsem,
            device_id=who, device_id_type=MESH,
        )
        copy.start()
        sent.append(copy)
        return copy

    m_ref[...] = jnp.full_like(m_ref, NEG)
    l_ref[...] = jnp.zeros_like(l_ref)
    acc[...] = jnp.zeros_like(acc)
    lanes = lax.broadcasted_iota(jnp.int32, (1, 64), 1)
    local[1].wait()
    own = (lanes == blocks_ref[b]).astype(F32)
    turn = lax.broadcasted_iota(jnp.int32, (256, 256), 0) == lax.broadcasted_iota(
        jnp.int32, (256, 256), 1
    )
    kbuf[0, 0:256, 0:576] = dot(turn.astype(F32).astype(BF16), k_in[...], NT).astype(BF16)
    kbuf[0, 0:256, 576:640] = jnp.broadcast_to(own, (256, 64)).astype(BF16)
    local[0].wait()
    qbuf[0, :, 0:576] = q_in[...]
    for i in range(8):
        seen = jnp.where(lanes >= reach_ref[i], F32(NEG), F32(0.0))
        qbuf[0, 32 * i : 32 * i + 32, 576:640] = jnp.broadcast_to(seen, (32, 64)).astype(BF16)

    pl.semaphore_wait(barrier, len(partners))

    quarter = pl.ds(pl.multiple_of(128 * p + 64 * c, 64), 64)
    quarter_x = pl.ds(pl.multiple_of(128 * (1 - p) + 64 * c, 64), 64)
    yp, ym = dev(y_=(y + 1) % 4), dev(y_=(y + 3) % 4)
    kz = {}

    def ring(r, xb, src, dst, s_sem, r_sem, table):
        forward = r <= 3 or (r == 4 and xb == 0)
        table[r, xb] = send(src, dst, s_sem.at[r, xb], r_sem.at[r, xb], zp if forward else zm)

    def k_rows(r, xb):
        return kbuf.at[r, 64 * xb : 64 * xb + 64]

    def q_send(n, s_from, s_to, half, who):
        rows = slice(128 * half, 128 * half + 128)
        return send(qbuf.at[s_from, rows], qbuf.at[s_to, rows], q_s.at[n], q_r.at[n], who)

    ox = [
        send(kbuf.at[0, quarter_x], kbuf.at[0, 256:320], kx_s.at[0, 0], kx_r.at[0, 0], other_x)
    ]
    for r in (1, 7):
        ring(r, 0, kbuf.at[0, quarter], k_rows(r, 0), kz_s, kz_r, kz)
    qp = [q_send(0, 0, 1, 0, yp)]
    qm = [q_send(1, 0, 3, 1, ym)]
    ox.append(
        send(kbuf.at[0, quarter], kbuf.at[0, 320:384], kx_s.at[0, 1], kx_r.at[0, 1], other_x)
    )
    qp.append(q_send(2, 0, 1, 1, yp))
    qm.append(q_send(3, 0, 3, 0, ym))

    local[2].wait()

    def suffix(i, carry):
        for n in range(4):
            rows = pl.ds(pl.multiple_of(i * 128 + n * 32, 32), 32)
            toks = pl.ds(pl.multiple_of(i * 256 + n * 64, 64), 64)
            sc = dot(qbuf[0, rows, 0:576], s_in[toks, :], NT) * C2
            sc = jnp.where(lanes < len_ref[4 * i + n], sc, F32(NEG))
            top = jnp.max(sc, axis=1, keepdims=True)
            weight = jnp.exp2(sc - top)
            m_ref[rows, :] = jnp.broadcast_to(top, (32, 128))
            l_ref[rows, :] = jnp.broadcast_to(jnp.sum(weight, axis=1, keepdims=True), (32, 128))
            start = dot(weight.astype(BF16), s_in[toks, 0:512], NN)
            for j in range(4):
                acc[j, rows, :] = start[:, 128 * j : 128 * j + 128]
        return carry

    lax.fori_loop(0, 2, suffix, 0)

    def score(s, r):
        return dot(qbuf[s], kbuf[r], NT)

    def fold(s, r, sc):
        rows = pl.ds(s * 256, 256)
        before = m_ref[rows, :]
        after = jnp.maximum(before, jnp.max(sc, axis=1, keepdims=True) * C2)
        shrink = jnp.exp2(before - after)
        weight = jnp.exp2(sc * C2 - after[:, :1])
        l_ref[rows, :] = l_ref[rows, :] * shrink + jnp.sum(weight, axis=1, keepdims=True)
        m_ref[rows, :] = after
        more = dot(weight.astype(BF16), kbuf[r, :, 0:512], NN)
        for j in range(4):
            acc[j, rows, :] = acc[j, rows, :] * shrink + more[:, 128 * j : 128 * j + 128]

    def attend(todo):
        now = score(*todo[0])
        for n, (s, r) in enumerate(todo):
            later = score(*todo[n + 1]) if n + 1 < len(todo) else None
            fold(s, r, now)
            now = later

    kx, kc = {}, {}

    def from_z(r, xb):
        kz[r, xb].wait_recv()
        if r in (1, 2):
            ring(r + 1, xb, k_rows(r, xb), k_rows(r + 1, xb), kz_s, kz_r, kz)
        elif r in (7, 6):
            ring(r - 1, xb, k_rows(r, xb), k_rows(r - 1, xb), kz_s, kz_r, kz)
        elif (r, xb) in ((3, 0), (5, 1)):
            ring(4, xb, k_rows(r, xb), k_rows(4, xb), kz_s, kz_r, kz)
        if xb == 0:
            kx[r] = (
                send(kbuf.at[r, 0:64], kbuf.at[r, 128:192], kx_s.at[r, 0], kx_r.at[r, 0], same_x),
                send(kbuf.at[r, 0:64], kbuf.at[r, 192:256], kx_s.at[r, 1], kx_r.at[r, 1], other_x),
            )
        else:
            kc[r] = [
                send(kbuf.at[r, 0:128], kbuf.at[r, 256:384], kc_s.at[r, 0], kc_r.at[r, 0], sib)
            ]

    def from_x(r):
        for copy in kx[r]:
            copy.wait_recv()
        kc[r].append(
            send(kbuf.at[r, 128:256], kbuf.at[r, 384:512], kc_s.at[r, 1], kc_r.at[r, 1], sib)
        )

    def ready(r):
        for copy in kc[r]:
            copy.wait_recv()

    ox[0].wait_recv()
    for r in (1, 7):
        ring(r, 1, kbuf.at[0, 256:320], k_rows(r, 1), kz_s, kz_r, kz)
    from_z(1, 0)
    from_z(7, 0)
    ox[1].wait_recv()
    sib0 = send(kbuf.at[0, 256:384], kbuf.at[0, 384:512], kc_s.at[0, 0], kc_r.at[0, 0], sib)
    qp[0].wait_recv()
    q2 = [q_send(4, 1, 2, 0, yp)]
    qm[0].wait_recv()
    q2.append(q_send(5, 3, 2, 1, ym))
    sib0.wait_recv()
    attend([(0, 0)])
    from_z(1, 1)
    from_z(7, 1)
    from_z(2, 0)
    from_z(6, 0)
    from_x(1)
    from_x(7)
    qp[1].wait_recv()
    qm[1].wait_recv()
    attend([(1, 0), (3, 0)])
    from_z(2, 1)
    from_z(6, 1)
    ready(1)
    ready(7)
    local[3].wait()
    ws = []
    for d in (2, 1, 3):
        to = (y + d) % 4
        cols = pl.ds(pl.multiple_of(1024 * to, 1024), 1024)
        ws.append(
            send(w_in.at[:, cols], wbuf.at[80 * d : 80 * d + 80], w_s.at[d], w_r.at[d], dev(y_=to))
        )
    attend([(0, 1), (1, 1), (3, 1)])
    from_z(3, 0)
    from_z(5, 0)
    from_x(2)
    from_x(6)
    attend([(0, 7), (1, 7), (3, 7)])
    from_z(3, 1)
    from_z(5, 1)
    ready(2)
    ready(6)
    for copy in q2:
        copy.wait_recv()
    attend([(2, 0), (2, 1), (2, 7)])
    from_x(3)
    from_x(5)
    from_z(4, 0)
    from_z(4, 1)
    attend([(0, 2), (1, 2), (2, 2), (3, 2)])
    from_x(4)
    ready(3)
    ready(5)
    ready(4)

    def last(i, carry):
        r = 3 + i
        attend([(0, r), (1, r), (2, r), (3, r)])
        return carry

    lax.fori_loop(0, 4, last, 0)
    wbuf[0:80, :] = w_in[:, pl.ds(pl.multiple_of(1024 * y, 1024), 1024)]

    local[4].wait()

    heads_out = []
    for d in (2, 1, 3, 0):
        to = (y + d) % 4

        def up(i, carry):
            for n in range(4):
                h = to * 8 + i * 4 + n
                parts, logs = [], []
                for a in range(4):
                    rows = pl.ds(((y + 4 - a) % 4) * 256 + h, 8, stride=32)
                    tot = l_ref[rows, :]
                    inv = 1.0 / tot
                    parts.append(
                        jnp.concatenate([acc[j, rows, :] * inv for j in range(4)], axis=1)
                    )
                    logs.append(m_ref[rows, :] + jnp.log2(tot))
                attn = jnp.concatenate(parts, axis=0).astype(BF16)
                place = pl.ds(pl.multiple_of(i * 128 + n * 32, 32), 32)
                hv_send[d, place, :] = dot(attn, uv[h], NN).astype(BF16)
                lse_full[d, place, :] = jnp.concatenate(logs, axis=0)
            return carry

        lax.fori_loop(0, 2, up, 0)
        lse_send[d] = lse_full[d].T[0:8, :]
        if d:
            heads_out.append(
                (
                    send(hv_send.at[d], hv_recv.at[d], a_s.at[d, 0], a_r.at[d, 0], dev(y_=to)),
                    send(lse_send.at[d], lse_recv.at[d], a_s.at[d, 1], a_r.at[d, 1], dev(y_=to)),
                )
            )
    for pair in heads_out:
        for copy in pair:
            copy.wait_recv()
    logs = [lse_send[0]] + [lse_recv[d] for d in (1, 2, 3)]
    best = jnp.maximum(jnp.maximum(logs[0], logs[1]), jnp.maximum(logs[2], logs[3]))
    part = [jnp.exp2(x - best) for x in logs]
    norm = 1.0 / (part[0] + part[1] + part[2] + part[3])
    total = None
    for d in range(4):
        share = jnp.concatenate([part[d] * norm] * 16, axis=0).T
        term = share * (hv_send[0] if d == 0 else hv_recv[d]).astype(F32)
        total = term if d == 0 else total + term
    total = total.astype(BF16)
    for h in range(8):
        units[0, 0, :, 128 * h : 128 * h + 128] = total[32 * h : 32 * h + 32, :]

    hz = {}
    hx = send(units.at[0, 0], units.at[0, 1], h_s.at[0, 0], h_r.at[0, 0], across)
    for r in (1, 7):
        ring(r, 0, units.at[0, 0], units.at[r, 0], h_s, h_r, hz)

    def place_unit(r, xb):
        base = (xh if xb == 0 else 1 - xh) * 256 + ((z + 8 - r) % 8) * 8
        unit = units[r, xb].astype(F32)
        for a in range(4):
            hv_all[pl.ds(pl.multiple_of(base + 64 * a, 8), 8), :] = unit[8 * a : 8 * a + 8, :]

    place_unit(0, 0)
    hx.wait_recv()
    for r in (1, 7):
        ring(r, 1, units.at[0, 1], units.at[r, 1], h_s, h_r, hz)
    place_unit(0, 1)
    for r in (1, 7, 2, 6, 3, 5, 4):
        for xb in (0, 1):
            hz[r, xb].wait_recv()
            if r in (1, 2):
                ring(r + 1, xb, units.at[r, xb], units.at[r + 1, xb], h_s, h_r, hz)
            elif r in (7, 6):
                ring(r - 1, xb, units.at[r, xb], units.at[r - 1, xb], h_s, h_r, hz)
            elif (r, xb) in ((3, 0), (5, 1)):
                ring(4, xb, units.at[r, xb], units.at[4, xb], h_s, h_r, hz)
        for xb in (0, 1):
            place_unit(r, xb)

    for copy in ws:
        copy.wait_recv()
    back = []
    for dh in (3, 2, 1, 0):
        h = peer(0, dh)[0]
        rows = pl.ds(pl.multiple_of(128 * h, 128), 128)
        out_send[dh] = dot(wbuf[...], hv_all[rows, :].astype(BF16), NT).astype(BF16)
        for d in (2, 1, 3, 0):
            if d or dh:
                n = 4 * d + dh
                back.append(
                    send(
                        out_send.at[dh, 80 * d : 80 * d + 80], rs.at[n],
                        rs_s.at[n], rs_r.at[n], peer(d, dh),
                    )
                )
    result = out_send[0, 0:80, :].astype(F32)
    for copy in back:
        copy.wait_recv()
    for n in range(1, 16):
        result = result + rs[n].astype(F32)
    out_ref[...] = result.astype(BF16)
    for copy in sent:
        copy.wait_send()


def per_device(
    queries, prefix_latent, suffix_latent, suffix_len, prefix_blocks, caption_reach, w_uv, w_out
):
    dma = pltpu.SemaphoreType.DMA
    return pl.pallas_call(
        kernel,
        out_shape=jax.ShapeDtypeStruct((80, 128), BF16),
        in_specs=[pl.BlockSpec(memory_space=pl.ANY)] * 5
        + [pl.BlockSpec(memory_space=pltpu.SMEM)] * 3,
        out_specs=pl.BlockSpec(memory_space=pltpu.VMEM),
        scratch_shapes=[
            pltpu.VMEM((256, 576), BF16),
            pltpu.VMEM((576, 256), BF16),
            pltpu.VMEM((512, 576), BF16),
            pltpu.VMEM((32, 512, 128), BF16),
            pltpu.VMEM((80, 4096), BF16),
            pltpu.VMEM((4, 256, 640), BF16),
            pltpu.VMEM((8, 512, 640), BF16),
            pltpu.VMEM((4, 1024, 128), F32),
            pltpu.VMEM((1024, 128), F32),
            pltpu.VMEM((1024, 128), F32),
            pltpu.VMEM((320, 1024), BF16),
            pltpu.VMEM((4, 256, 128), BF16),
            pltpu.VMEM((4, 256, 128), F32),
            pltpu.VMEM((4, 8, 256), F32),
            pltpu.VMEM((4, 256, 128), BF16),
            pltpu.VMEM((4, 8, 256), F32),
            pltpu.VMEM((8, 2, 32, 1024), BF16),
            pltpu.VMEM((512, 1024), F32),
            pltpu.VMEM((4, 320, 128), BF16),
            pltpu.VMEM((16, 80, 128), BF16),
            dma((5,)),
            dma((8, 2)), dma((8, 2)),
            dma((8, 2)), dma((8, 2)),
            dma((8, 2)), dma((8, 2)),
            dma((6,)), dma((6,)),
            dma((4,)), dma((4,)),
            dma((4, 2)), dma((4, 2)),
            dma((8, 2)), dma((8, 2)),
            dma((16,)), dma((16,)),
        ],
        compiler_params=pltpu.CompilerParams(
            collective_id=0, has_side_effects=True, vmem_limit_bytes=56 * 2**20
        ),
    )(
        queries.reshape(256, 576),
        prefix_latent.T,
        suffix_latent.reshape(512, 576),
        w_uv,
        w_out.T,
        suffix_len,
        prefix_blocks,
        caption_reach,
    ).T


def solution(mesh):
    placed = (
        P("blk", "heads", None),
        P("blk", None),
        P("blk", None, None),
        P("blk"),
        P(),
        P("blk"),
        P("heads", None, None),
        P("heads", "blk"),
    )
    return jax.shard_map(
        per_device, mesh=mesh, in_specs=placed, out_specs=P("heads", "blk"), check_vma=False
    )
```

time: 98.6 us -> 79 us (0.80)
  Pallas kernels: 91.7 us -> 76.2 us
  local copies, waits for them, and re-layouts: 5.54 us -> 1.34 us
    pallas_call x1, Pallas kernels: 91.7 us -> 76.2 us  [per_device(): pl.pallas_call(kernel, out_shape=jax.ShapeDtypeStruct((80, 128), BF16), i...]
    unnamed x2 -> x1, local copies, waits for them, and re-layouts: 4.09 us -> 1.34 us
    pallas_call x1 -> x0, local copies, waits for them, and re-layouts: 1.45 us -> none  [per_device(): pl.pallas_call(kernel, out_shape=jax.ShapeDtypeStruct((128, 80), BF16), i...]
where the time goes in v2:
time: 79 us; the launch traced here: 77.6 us
  Pallas kernels  76.2 us (96%)
  local copies, waits for them, and re-layouts  1.34 us (2%)
    pallas_call x1, Pallas kernels, per_device(): pl.pallas_call(kernel, out_shape=jax.ShapeDtypeStruct((80, 128), BF16), i...  76.2 us

profile of v2, /device:TPU:2, one launch (start us, length us, event | category | flops | bytes accessed | tf_op | source)
XLA Modules:
  0.0 77.6 jit_solution(13324827071831266186)
XLA Ops:
  0.0 76.2 %shard_map.82 = bf16[80,128]{1,0:T(8,128)(2,1)} custom-call(bf16[256,576]{1,0:T(8,128)(2,1)} %bitcast.7, bf16[576,256]{1,0:T(8,128)(2,1)} %bitcast.8, bf16[512,576]{1,0:T(8,128)(2,1)} %bitcast.5, bf16[32,512,128]{2,1,0:T(8,128)(2,1)} %uv_hbm.1, bf16[80,4096]{1,0:T(8,128)(2,1)} %bitcast.6, s32[8]{0:T(128)} %len_ref.1, s32[64]{0:T(128)} %blocks_ref.1, s32[8]{0:T(128)} %reach_ref.1), custom_call_target="tpu_custom_call" | custom-call | tf_op jit(solution)/shard_map/pallas_call | solution.py:371
  76.2 1.3 %copy.10 = bf16[128,80]{0,1:T(8,128)(2,1)} copy(bf16[128,80]{0,1:T(8,128)(2,1)} %bitcast.9) | data formatting | bytes 40960

commit v3 on v2

--- a/solution.py
+++ b/solution.py
@@ -25,7 +25,7 @@
     wbuf, hv_send, lse_full, lse_send, hv_recv, lse_recv,
     units, hv_all, out_send, rs,
     in_sem, kz_s, kz_r, kx_s, kx_r, kc_s, kc_r, q_s, q_r, w_s, w_r,
-    a_s, a_r, h_s, h_r, rs_s, rs_r,
+    a_s, a_r, h_s, h_r, hx_s, hx_r, rs_s, rs_r,
 ):
     hd = lax.axis_index("heads")
     b = lax.axis_index("blk")
@@ -141,7 +141,6 @@
                 acc[j, rows, :] = start[:, 128 * j : 128 * j + 128]
         return carry
 
-    lax.fori_loop(0, 2, suffix, 0)
 
     def score(s, r):
         return dot(qbuf[s], kbuf[r], NT)
@@ -207,21 +206,26 @@
     q2 = [q_send(4, 1, 2, 0, yp)]
     qm[0].wait_recv()
     q2.append(q_send(5, 3, 2, 1, ym))
+    lax.fori_loop(0, 2, suffix, 0)
     sib0.wait_recv()
     attend([(0, 0)])
-    from_z(1, 1)
-    from_z(7, 1)
-    from_z(2, 0)
-    from_z(6, 0)
+    for part in ((1, 1), (7, 1), (2, 0), (6, 0)):
+        from_z(*part)
     from_x(1)
     from_x(7)
     qp[1].wait_recv()
     qm[1].wait_recv()
     attend([(1, 0), (3, 0)])
-    from_z(2, 1)
-    from_z(6, 1)
     ready(1)
     ready(7)
+    attend([(0, 1), (1, 1), (3, 1)])
+    for part in ((2, 1), (6, 1), (3, 0), (5, 0)):
+        from_z(*part)
+    from_x(2)
+    from_x(6)
+    attend([(0, 7), (1, 7), (3, 7)])
+    for copy in q2:
+        copy.wait_recv()
     local[3].wait()
     ws = []
     for d in (2, 1, 3):
@@ -230,46 +234,38 @@
         ws.append(
             send(w_in.at[:, cols], wbuf.at[80 * d : 80 * d + 80], w_s.at[d], w_r.at[d], dev(y_=to))
         )
-    attend([(0, 1), (1, 1), (3, 1)])
-    from_z(3, 0)
-    from_z(5, 0)
-    from_x(2)
-    from_x(6)
-    attend([(0, 7), (1, 7), (3, 7)])
-    from_z(3, 1)
-    from_z(5, 1)
+    attend([(2, 0), (2, 1), (2, 7)])
+    for part in ((3, 1), (5, 1), (4, 0)):
+        from_z(*part)
     ready(2)
     ready(6)
-    for copy in q2:
-        copy.wait_recv()
-    attend([(2, 0), (2, 1), (2, 7)])
+    attend([(0, 2), (1, 2), (2, 2), (3, 2)])
     from_x(3)
     from_x(5)
-    from_z(4, 0)
     from_z(4, 1)
-    attend([(0, 2), (1, 2), (2, 2), (3, 2)])
     from_x(4)
     ready(3)
     ready(5)
-    ready(4)
 
     def last(i, carry):
-        r = 3 + i
+        r = jnp.where(i == 0, 6, 1 + 2 * i)
         attend([(0, r), (1, r), (2, r), (3, r)])
         return carry
 
-    lax.fori_loop(0, 4, last, 0)
+    lax.fori_loop(0, 3, last, 0)
+    ready(4)
+    attend([(0, 4), (1, 4), (2, 4), (3, 4)])
     wbuf[0:80, :] = w_in[:, pl.ds(pl.multiple_of(1024 * y, 1024), 1024)]
 
     local[4].wait()
 
-    heads_out = []
-    for d in (2, 1, 3, 0):
-        to = (y + d) % 4
-
-        def up(i, carry):
+    heads_out = {}
+    for half in (0, 1):
+        heads_out[half] = []
+        for d in (2, 1, 3, 0):
+            to = (y + d) % 4
             for n in range(4):
-                h = to * 8 + i * 4 + n
+                h = to * 8 + half * 4 + n
                 parts, logs = [], []
                 for a in range(4):
                     rows = pl.ds(((y + 4 - a) % 4) * 256 + h, 8, stride=32)
@@ -280,63 +276,84 @@
                     )
                     logs.append(m_ref[rows, :] + jnp.log2(tot))
                 attn = jnp.concatenate(parts, axis=0).astype(BF16)
-                place = pl.ds(pl.multiple_of(i * 128 + n * 32, 32), 32)
-                hv_send[d, place, :] = dot(attn, uv[h], NN).astype(BF16)
-                lse_full[d, place, :] = jnp.concatenate(logs, axis=0)
-            return carry
-
-        lax.fori_loop(0, 2, up, 0)
-        lse_send[d] = lse_full[d].T[0:8, :]
-        if d:
-            heads_out.append(
-                (
-                    send(hv_send.at[d], hv_recv.at[d], a_s.at[d, 0], a_r.at[d, 0], dev(y_=to)),
-                    send(lse_send.at[d], lse_recv.at[d], a_s.at[d, 1], a_r.at[d, 1], dev(y_=to)),
-                )
-            )
-    for pair in heads_out:
-        for copy in pair:
+                hv_send[d, half, 32 * n : 32 * n + 32, :] = dot(attn, uv[h], NN).astype(BF16)
+                lse_full[32 * n : 32 * n + 32, :] = jnp.concatenate(logs, axis=0)
+            lse_send[d, half] = lse_full[...].T[0:8, :]
+            if d:
+                n = 2 * half
+                who = dev(y_=to)
+                heads_out[half] += [
+                    send(hv_send.at[d, half], hv_recv.at[d, half], a_s.at[d, n], a_r.at[d, n], who),
+                    send(
+                        lse_send.at[d, half], lse_recv.at[d, half],
+                        a_s.at[d, n + 1], a_r.at[d, n + 1], who,
+                    ),
+                ]
+
+    hz, hx = {}, {}
+
+    def z_ring(r, half, start):
+        forward = r <= 3 or (r == 4 and half == 0)
+        hz[r, half] = send(
+            units.at[start, 0, half], units.at[r, 0, half],
+            h_s.at[r, half], h_r.at[r, half], zp if forward else zm,
+        )
+
+    def cross(r, half):
+        hx[r, half] = send(
+            units.at[r, 0, half], units.at[r, 1, half], hx_s.at[r, half], hx_r.at[r, half], across
+        )
+
+    def place_unit(r, xb, half):
+        base = (xh if xb == 0 else 1 - xh) * 256 + ((z + 8 - r) % 8) * 8
+        unit = units[r, xb, half].astype(F32)
+        for a in range(4):
+            rows = pl.ds(pl.multiple_of(base + 64 * a, 8), 8)
+            hv_all[rows, 512 * half : 512 * half + 512] = unit[8 * a : 8 * a + 8, :]
+
+    for half in (0, 1):
+        for copy in heads_out[half]:
             copy.wait_recv()
-    logs = [lse_send[0]] + [lse_recv[d] for d in (1, 2, 3)]
-    best = jnp.maximum(jnp.maximum(logs[0], logs[1]), jnp.maximum(logs[2], logs[3]))
-    part = [jnp.exp2(x - best) for x in logs]
-    norm = 1.0 / (part[0] + part[1] + part[2] + part[3])
-    total = None
-    for d in range(4):
-        share = jnp.concatenate([part[d] * norm] * 16, axis=0).T
-        term = share * (hv_send[0] if d == 0 else hv_recv[d]).astype(F32)
-        total = term if d == 0 else total + term
-    total = total.astype(BF16)
-    for h in range(8):
-        units[0, 0, :, 128 * h : 128 * h + 128] = total[32 * h : 32 * h + 32, :]
-
-    hz = {}
-    hx = send(units.at[0, 0], units.at[0, 1], h_s.at[0, 0], h_r.at[0, 0], across)
-    for r in (1, 7):
-        ring(r, 0, units.at[0, 0], units.at[r, 0], h_s, h_r, hz)
-
-    def place_unit(r, xb):
-        base = (xh if xb == 0 else 1 - xh) * 256 + ((z + 8 - r) % 8) * 8
-        unit = units[r, xb].astype(F32)
-        for a in range(4):
-            hv_all[pl.ds(pl.multiple_of(base + 64 * a, 8), 8), :] = unit[8 * a : 8 * a + 8, :]
-
-    place_unit(0, 0)
-    hx.wait_recv()
-    for r in (1, 7):
-        ring(r, 1, units.at[0, 1], units.at[r, 1], h_s, h_r, hz)
-    place_unit(0, 1)
-    for r in (1, 7, 2, 6, 3, 5, 4):
-        for xb in (0, 1):
-            hz[r, xb].wait_recv()
-            if r in (1, 2):
-                ring(r + 1, xb, units.at[r, xb], units.at[r + 1, xb], h_s, h_r, hz)
-            elif r in (7, 6):
-                ring(r - 1, xb, units.at[r, xb], units.at[r - 1, xb], h_s, h_r, hz)
-            elif (r, xb) in ((3, 0), (5, 1)):
-                ring(4, xb, units.at[r, xb], units.at[4, xb], h_s, h_r, hz)
-        for xb in (0, 1):
-            place_unit(r, xb)
+        logs = [lse_send[0, half]] + [lse_recv[d, half] for d in (1, 2, 3)]
+        best = jnp.maximum(jnp.maximum(logs[0], logs[1]), jnp.maximum(logs[2], logs[3]))
+        part = [jnp.exp2(x - best) for x in logs]
+        norm = 1.0 / (part[0] + part[1] + part[2] + part[3])
+        share = [jnp.concatenate([x * norm] * 16, axis=0).T for x in part]
+        total = share[0] * hv_send[0, half].astype(F32)
+        for d in (1, 2, 3):
+            total = total + share[d] * hv_recv[d, half].astype(F32)
+        total = total.astype(BF16)
+        for h in range(4):
+            units[0, 0, half, :, 128 * h : 128 * h + 128] = total[32 * h : 32 * h + 32, :]
+        z_ring(1, half, 0)
+        z_ring(7, half, 0)
+        cross(0, half)
+    place_unit(0, 0, 0)
+    place_unit(0, 0, 1)
+    before = [(0, 0), (0, 1)]
+    for pair in ((1, 7), (2, 6), (3, 5), (4,)):
+        for half in (0, 1):
+            for r in pair:
+                hz[r, half].wait_recv()
+                if r in (1, 2):
+                    z_ring(r + 1, half, r)
+                elif r in (7, 6):
+                    z_ring(r - 1, half, r)
+                elif (r, half) in ((3, 0), (5, 1)):
+                    z_ring(4, half, r)
+                cross(r, half)
+        for r in pair:
+            place_unit(r, 0, 0)
+            place_unit(r, 0, 1)
+        if pair[0] > 1:
+            for r, half in before:
+                hx[r, half].wait_recv()
+                place_unit(r, 1, half)
+            before = []
+        before += [(r, half) for r in pair for half in (0, 1)]
+    for r, half in before:
+        hx[r, half].wait_recv()
+        place_unit(r, 1, half)
 
     for copy in ws:
         copy.wait_recv()
@@ -386,12 +403,12 @@
             pltpu.VMEM((1024, 128), F32),
             pltpu.VMEM((1024, 128), F32),
             pltpu.VMEM((320, 1024), BF16),
-            pltpu.VMEM((4, 256, 128), BF16),
-            pltpu.VMEM((4, 256, 128), F32),
-            pltpu.VMEM((4, 8, 256), F32),
-            pltpu.VMEM((4, 256, 128), BF16),
-            pltpu.VMEM((4, 8, 256), F32),
-            pltpu.VMEM((8, 2, 32, 1024), BF16),
+            pltpu.VMEM((4, 2, 128, 128), BF16),
+            pltpu.VMEM((128, 128), F32),
+            pltpu.VMEM((4, 2, 8, 128), F32),
+            pltpu.VMEM((4, 2, 128, 128), BF16),
+            pltpu.VMEM((4, 2, 8, 128), F32),
+            pltpu.VMEM((8, 2, 2, 32, 512), BF16),
             pltpu.VMEM((512, 1024), F32),
             pltpu.VMEM((4, 320, 128), BF16),
             pltpu.VMEM((16, 80, 128), BF16),
@@ -401,7 +418,8 @@
             dma((8, 2)), dma((8, 2)),
             dma((6,)), dma((6,)),
             dma((4,)), dma((4,)),
-            dma((4, 2)), dma((4, 2)),
+            dma((4, 4)), dma((4, 4)),
+            dma((8, 2)), dma((8, 2)),
             dma((8, 2)), dma((8, 2)),
             dma((16,)), dma((16,)),
         ],

time: 79 us -> 74.3 us (0.941)
  Pallas kernels: 76.2 us -> 72 us
    pallas_call x1, Pallas kernels: 76.2 us -> 72 us  [per_device(): pl.pallas_call(kernel, out_shape=jax.ShapeDtypeStruct((80, 128), BF16), i...]
where the time goes in v3:
time: 74.3 us; the launch traced here: 73.3 us
  Pallas kernels  72 us (97%)
  local copies, waits for them, and re-layouts  1.34 us (2%)
    pallas_call x1, Pallas kernels, per_device(): pl.pallas_call(kernel, out_shape=jax.ShapeDtypeStruct((80, 128), BF16), i...  72 us

profile of v3, /device:TPU:2, one launch (start us, length us, event | category | flops | bytes accessed | tf_op | source)
XLA Modules:
  0.0 73.3 jit_solution(15302018179171071211)
XLA Ops:
  0.0 72.0 %shard_map.82 = bf16[80,128]{1,0:T(8,128)(2,1)} custom-call(bf16[256,576]{1,0:T(8,128)(2,1)} %bitcast.7, bf16[576,256]{1,0:T(8,128)(2,1)} %bitcast.8, bf16[512,576]{1,0:T(8,128)(2,1)} %bitcast.5, bf16[32,512,128]{2,1,0:T(8,128)(2,1)} %uv_hbm.1, bf16[80,4096]{1,0:T(8,128)(2,1)} %bitcast.6, s32[8]{0:T(128)} %len_ref.1, s32[64]{0:T(128)} %blocks_ref.1, s32[8]{0:T(128)} %reach_ref.1), custom_call_target="tpu_custom_call" | custom-call | tf_op jit(solution)/shard_map/pallas_call | solution.py:388
  72.0 1.3 %copy.10 = bf16[128,80]{0,1:T(8,128)(2,1)} copy(bf16[128,80]{0,1:T(8,128)(2,1)} %bitcast.9) | data formatting | bytes 40960

commit v4 on v3

--- a/solution.py
+++ b/solution.py
@@ -59,7 +59,7 @@
         copy.start()
         local.append(copy)
 
-    partners = [zp, zm, other_x, across]
+    partners = [zp, zm, dev(z_=(z + 2) % 8), dev(z_=(z + 6) % 8), other_x, across]
     partners += [peer(d, dh) for d in range(4) for dh in range(4) if d or dh]
     barrier = pltpu.get_barrier_semaphore()
     for who in partners:
@@ -95,31 +95,43 @@
 
     pl.semaphore_wait(barrier, len(partners))
 
-    quarter = pl.ds(pl.multiple_of(128 * p + 64 * c, 64), 64)
-    quarter_x = pl.ds(pl.multiple_of(128 * (1 - p) + 64 * c, 64), 64)
+    def quarter(mine, piece):
+        start = 128 * (p if mine else 1 - p) + 64 * c + 32 * piece
+        return kbuf.at[0, pl.ds(pl.multiple_of(start, 32), 32)]
+
     yp, ym = dev(y_=(y + 1) % 4), dev(y_=(y + 3) % 4)
     kz = {}
 
-    def ring(r, xb, src, dst, s_sem, r_sem, table):
+    def k_rows(r, xb, piece):
+        start = 32 * piece + (256 if r == 0 else 64 * xb)
+        return kbuf.at[r, start : start + 32]
+
+    def ring(r, xb, piece, src):
         forward = r <= 3 or (r == 4 and xb == 0)
-        table[r, xb] = send(src, dst, s_sem.at[r, xb], r_sem.at[r, xb], zp if forward else zm)
-
-    def k_rows(r, xb):
-        return kbuf.at[r, 64 * xb : 64 * xb + 64]
+        n = 2 * xb + piece
+        kz[r, xb, piece] = send(
+            src, k_rows(r, xb, piece), kz_s.at[r, n], kz_r.at[r, n], zp if forward else zm
+        )
 
     def q_send(n, s_from, s_to, half, who):
         rows = slice(128 * half, 128 * half + 128)
         return send(qbuf.at[s_from, rows], qbuf.at[s_to, rows], q_s.at[n], q_r.at[n], who)
 
-    ox = [
-        send(kbuf.at[0, quarter_x], kbuf.at[0, 256:320], kx_s.at[0, 0], kx_r.at[0, 0], other_x)
-    ]
-    for r in (1, 7):
-        ring(r, 0, kbuf.at[0, quarter], k_rows(r, 0), kz_s, kz_r, kz)
+    ox = []
+    for piece in (0, 1):
+        ox.append(
+            send(
+                quarter(False, piece), k_rows(0, 1, piece),
+                kx_s.at[0, piece], kx_r.at[0, piece], other_x,
+            )
+        )
+        for r in (1, 7):
+            ring(r, 0, piece, quarter(True, piece))
     qp = [q_send(0, 0, 1, 0, yp)]
     qm = [q_send(1, 0, 3, 1, ym)]
+    whole = pl.ds(pl.multiple_of(128 * p + 64 * c, 64), 64)
     ox.append(
-        send(kbuf.at[0, quarter], kbuf.at[0, 320:384], kx_s.at[0, 1], kx_r.at[0, 1], other_x)
+        send(kbuf.at[0, whole], kbuf.at[0, 320:384], kx_s.at[0, 2], kx_r.at[0, 2], other_x)
     )
     qp.append(q_send(2, 0, 1, 1, yp))
     qm.append(q_send(3, 0, 3, 0, ym))
@@ -166,23 +178,27 @@
 
     kx, kc = {}, {}
 
-    def from_z(r, xb):
-        kz[r, xb].wait_recv()
-        if r in (1, 2):
-            ring(r + 1, xb, k_rows(r, xb), k_rows(r + 1, xb), kz_s, kz_r, kz)
-        elif r in (7, 6):
-            ring(r - 1, xb, k_rows(r, xb), k_rows(r - 1, xb), kz_s, kz_r, kz)
-        elif (r, xb) in ((3, 0), (5, 1)):
-            ring(4, xb, k_rows(r, xb), k_rows(4, xb), kz_s, kz_r, kz)
-        if xb == 0:
-            kx[r] = (
-                send(kbuf.at[r, 0:64], kbuf.at[r, 128:192], kx_s.at[r, 0], kx_r.at[r, 0], same_x),
-                send(kbuf.at[r, 0:64], kbuf.at[r, 192:256], kx_s.at[r, 1], kx_r.at[r, 1], other_x),
-            )
-        else:
-            kc[r] = [
-                send(kbuf.at[r, 0:128], kbuf.at[r, 256:384], kc_s.at[r, 0], kc_r.at[r, 0], sib)
-            ]
+    def from_z(*parts):
+        for piece in (0, 1):
+            for r, xb in parts:
+                kz[r, xb, piece].wait_recv()
+                if r in (1, 2):
+                    ring(r + 1, xb, piece, k_rows(r, xb, piece))
+                elif r in (7, 6):
+                    ring(r - 1, xb, piece, k_rows(r, xb, piece))
+                elif (r, xb) in ((3, 0), (5, 1)):
+                    ring(4, xb, piece, k_rows(r, xb, piece))
+        for r, xb in parts:
+            if xb == 0:
+                half = kbuf.at[r, 0:64]
+                kx[r] = (
+                    send(half, kbuf.at[r, 128:192], kx_s.at[r, 0], kx_r.at[r, 0], same_x),
+                    send(half, kbuf.at[r, 192:256], kx_s.at[r, 1], kx_r.at[r, 1], other_x),
+                )
+            else:
+                kc[r] = [
+                    send(kbuf.at[r, 0:128], kbuf.at[r, 256:384], kc_s.at[r, 0], kc_r.at[r, 0], sib)
+                ]
 
     def from_x(r):
         for copy in kx[r]:
@@ -195,37 +211,38 @@
         for copy in kc[r]:
             copy.wait_recv()
 
-    ox[0].wait_recv()
-    for r in (1, 7):
-        ring(r, 1, kbuf.at[0, 256:320], k_rows(r, 1), kz_s, kz_r, kz)
-    from_z(1, 0)
-    from_z(7, 0)
-    ox[1].wait_recv()
+    for piece in (0, 1):
+        ox[piece].wait_recv()
+        for r in (1, 7):
+            ring(r, 1, piece, k_rows(0, 1, piece))
+    from_z((1, 0), (7, 0))
+    ox[2].wait_recv()
     sib0 = send(kbuf.at[0, 256:384], kbuf.at[0, 384:512], kc_s.at[0, 0], kc_r.at[0, 0], sib)
     qp[0].wait_recv()
     q2 = [q_send(4, 1, 2, 0, yp)]
     qm[0].wait_recv()
     q2.append(q_send(5, 3, 2, 1, ym))
     lax.fori_loop(0, 2, suffix, 0)
+    from_z((1, 1), (7, 1))
     sib0.wait_recv()
     attend([(0, 0)])
-    for part in ((1, 1), (7, 1), (2, 0), (6, 0)):
-        from_z(*part)
+    from_z((2, 0), (6, 0))
     from_x(1)
     from_x(7)
     qp[1].wait_recv()
     qm[1].wait_recv()
     attend([(1, 0), (3, 0)])
+    from_z((2, 1), (6, 1))
     ready(1)
     ready(7)
     attend([(0, 1), (1, 1), (3, 1)])
-    for part in ((2, 1), (6, 1), (3, 0), (5, 0)):
-        from_z(*part)
+    from_z((3, 0), (5, 0))
     from_x(2)
     from_x(6)
     attend([(0, 7), (1, 7), (3, 7)])
     for copy in q2:
         copy.wait_recv()
+    from_z((3, 1), (5, 1))
     local[3].wait()
     ws = []
     for d in (2, 1, 3):
@@ -235,24 +252,19 @@
             send(w_in.at[:, cols], wbuf.at[80 * d : 80 * d + 80], w_s.at[d], w_r.at[d], dev(y_=to))
         )
     attend([(2, 0), (2, 1), (2, 7)])
-    for part in ((3, 1), (5, 1), (4, 0)):
-        from_z(*part)
+    from_z((4, 0))
     ready(2)
     ready(6)
     attend([(0, 2), (1, 2), (2, 2), (3, 2)])
     from_x(3)
     from_x(5)
-    from_z(4, 1)
+    from_z((4, 1))
+    attend([(0, 6), (1, 6), (2, 6), (3, 6)])
+    ready(3)
+    attend([(0, 3), (1, 3), (2, 3), (3, 3)])
     from_x(4)
-    ready(3)
     ready(5)
-
-    def last(i, carry):
-        r = jnp.where(i == 0, 6, 1 + 2 * i)
-        attend([(0, r), (1, r), (2, r), (3, r)])
-        return carry
-
-    lax.fori_loop(0, 3, last, 0)
+    attend([(0, 5), (1, 5), (2, 5), (3, 5)])
     ready(4)
     attend([(0, 4), (1, 4), (2, 4), (3, 4)])
     wbuf[0:80, :] = w_in[:, pl.ds(pl.multiple_of(1024 * y, 1024), 1024)]
@@ -292,11 +304,12 @@
 
     hz, hx = {}, {}
 
-    def z_ring(r, half, start):
-        forward = r <= 3 or (r == 4 and half == 0)
+    def along_z(r, half, start):
+        steps = (r - start) % 8
+        who = dev(z_=(z + steps) % 8)
         hz[r, half] = send(
             units.at[start, 0, half], units.at[r, 0, half],
-            h_s.at[r, half], h_r.at[r, half], zp if forward else zm,
+            h_s.at[r, half], h_r.at[r, half], who,
         )
 
     def cross(r, half):
@@ -325,33 +338,40 @@
         total = total.astype(BF16)
         for h in range(4):
             units[0, 0, half, :, 128 * h : 128 * h + 128] = total[32 * h : 32 * h + 32, :]
-        z_ring(1, half, 0)
-        z_ring(7, half, 0)
+        for r in (2, 6, 1, 7):
+            along_z(r, half, 0)
         cross(0, half)
     place_unit(0, 0, 0)
     place_unit(0, 0, 1)
-    before = [(0, 0), (0, 1)]
-    for pair in ((1, 7), (2, 6), (3, 5), (4,)):
+    done = 0
+    while done < len(sent) and sent[done] is not hz[2, 0]:
+        sent[done].wait_send()
+        done += 1
+    for half in (0, 1):
+        for r in (1, 7, 2, 6):
+            hz[r, half].wait_recv()
+            if r == 2:
+                along_z(3, half, 2)
+                if half == 0:
+                    along_z(4, half, 2)
+            elif r == 6:
+                along_z(5, half, 6)
+                if half == 1:
+                    along_z(4, half, 6)
+            cross(r, half)
+    for r in (1, 7, 2, 6):
         for half in (0, 1):
-            for r in pair:
-                hz[r, half].wait_recv()
-                if r in (1, 2):
-                    z_ring(r + 1, half, r)
-                elif r in (7, 6):
-                    z_ring(r - 1, half, r)
-                elif (r, half) in ((3, 0), (5, 1)):
-                    z_ring(4, half, r)
-                cross(r, half)
-        for r in pair:
-            place_unit(r, 0, 0)
-            place_unit(r, 0, 1)
-        if pair[0] > 1:
-            for r, half in before:
-                hx[r, half].wait_recv()
-                place_unit(r, 1, half)
-            before = []
-        before += [(r, half) for r in pair for half in (0, 1)]
-    for r, half in before:
+            place_unit(r, 0, half)
+    for r, half in ((0, 0), (0, 1), (1, 0), (7, 0)):
+        hx[r, half].wait_recv()
+        place_unit(r, 1, half)
+    for r, half in ((3, 0), (5, 0), (4, 0), (3, 1), (5, 1), (4, 1)):
+        hz[r, half].wait_recv()
+        cross(r, half)
+        place_unit(r, 0, half)
+    for r, half in (
+        (2, 0), (6, 0), (1, 1), (7, 1), (2, 1), (6, 1), (3, 0), (5, 0), (4, 0), (3, 1), (5, 1), (4, 1)
+    ):
         hx[r, half].wait_recv()
         place_unit(r, 1, half)
 
@@ -372,12 +392,14 @@
                     )
                 )
     result = out_send[0, 0:80, :].astype(F32)
+    for copy in sent[done : len(sent) - len(back)]:
+        copy.wait_send()
     for copy in back:
         copy.wait_recv()
     for n in range(1, 16):
         result = result + rs[n].astype(F32)
     out_ref[...] = result.astype(BF16)
-    for copy in sent:
+    for copy in back:
         copy.wait_send()
 
 
@@ -413,8 +435,8 @@
             pltpu.VMEM((4, 320, 128), BF16),
             pltpu.VMEM((16, 80, 128), BF16),
             dma((5,)),
-            dma((8, 2)), dma((8, 2)),
-            dma((8, 2)), dma((8, 2)),
+            dma((8, 4)), dma((8, 4)),
+            dma((8, 3)), dma((8, 3)),
             dma((8, 2)), dma((8, 2)),
             dma((6,)), dma((6,)),
             dma((4,)), dma((4,)),

time: 74.3 us -> 70.1 us (0.943)
  Pallas kernels: 72 us -> 67.7 us
    pallas_call x1, Pallas kernels: 72 us -> 67.7 us  [per_device(): pl.pallas_call(kernel, out_shape=jax.ShapeDtypeStruct((80, 128), BF16), i...]
where the time goes in v4:
time: 70.1 us; the launch traced here: 69 us
  Pallas kernels  67.7 us (97%)
  local copies, waits for them, and re-layouts  1.34 us (2%)
    pallas_call x1, Pallas kernels, per_device(): pl.pallas_call(kernel, out_shape=jax.ShapeDtypeStruct((80, 128), BF16), i...  67.7 us

profile of v4, /device:TPU:2, one launch (start us, length us, event | category | flops | bytes accessed | tf_op | source)
XLA Modules:
  0.0 69.0 jit_solution(17310401642795128186)
XLA Ops:
  0.0 67.7 %shard_map.82 = bf16[80,128]{1,0:T(8,128)(2,1)} custom-call(bf16[256,576]{1,0:T(8,128)(2,1)} %bitcast.7, bf16[576,256]{1,0:T(8,128)(2,1)} %bitcast.8, bf16[512,576]{1,0:T(8,128)(2,1)} %bitcast.5, bf16[32,512,128]{2,1,0:T(8,128)(2,1)} %uv_hbm.1, bf16[80,4096]{1,0:T(8,128)(2,1)} %bitcast.6, s32[8]{0:T(128)} %len_ref.1, s32[64]{0:T(128)} %blocks_ref.1, s32[8]{0:T(128)} %reach_ref.1), custom_call_target="tpu_custom_call" | custom-call | tf_op jit(solution)/shard_map/pallas_call | solution.py:410
  67.7 1.3 %copy.10 = bf16[128,80]{0,1:T(8,128)(2,1)} copy(bf16[128,80]{0,1:T(8,128)(2,1)} %bitcast.9) | data formatting | bytes 40960

commit v5 on v4

--- a/solution.py
+++ b/solution.py
@@ -312,6 +312,12 @@
             h_s.at[r, half], h_r.at[r, half], who,
         )
 
+    def crossed_along_z(r, half, start):
+        hx[r, half] = send(
+            units.at[start, 1, half], units.at[r, 1, half],
+            hx_s.at[r, half], hx_r.at[r, half], zp if r in (1, 3) else zm,
+        )
+
     def cross(r, half):
         hx[r, half] = send(
             units.at[r, 0, half], units.at[r, 1, half], hx_s.at[r, half], hx_r.at[r, half], across
@@ -358,19 +364,33 @@
                 along_z(5, half, 6)
                 if half == 1:
                     along_z(4, half, 6)
-            cross(r, half)
+            if r in (2, 6):
+                cross(r, half)
+    for half in (0, 1):
+        hx[0, half].wait_recv()
+        for r in (1, 7):
+            crossed_along_z(r, half, 0)
     for r in (1, 7, 2, 6):
         for half in (0, 1):
             place_unit(r, 0, half)
-    for r, half in ((0, 0), (0, 1), (1, 0), (7, 0)):
-        hx[r, half].wait_recv()
-        place_unit(r, 1, half)
-    for r, half in ((3, 0), (5, 0), (4, 0), (3, 1), (5, 1), (4, 1)):
+    for half in (0, 1):
+        place_unit(0, 1, half)
+    for half in (0, 1):
+        hx[2, half].wait_recv()
+        crossed_along_z(3, half, 2)
+        hx[6, half].wait_recv()
+        crossed_along_z(5, half, 6)
+        hz[4, half].wait_recv()
+        cross(4, half)
+        for r in (2, 6):
+            place_unit(r, 1, half)
+    for r, half in ((4, 0), (4, 1)):
+        place_unit(r, 0, half)
+    for r, half in ((3, 0), (5, 0), (3, 1), (5, 1)):
         hz[r, half].wait_recv()
-        cross(r, half)
         place_unit(r, 0, half)
     for r, half in (
-        (2, 0), (6, 0), (1, 1), (7, 1), (2, 1), (6, 1), (3, 0), (5, 0), (4, 0), (3, 1), (5, 1), (4, 1)
+        (1, 0), (7, 0), (1, 1), (7, 1), (3, 0), (5, 0), (4, 0), (3, 1), (5, 1), (4, 1)
     ):
         hx[r, half].wait_recv()
         place_unit(r, 1, half)

time: 70.1 us -> 69.5 us (level)
  no operation moved by 1% of the time
where the time goes in v5:
time: 69.5 us; the launch traced here: 68.6 us
  Pallas kernels  67.2 us (97%)
  local copies, waits for them, and re-layouts  1.34 us (2%)
    pallas_call x1, Pallas kernels, per_device(): pl.pallas_call(kernel, out_shape=jax.ShapeDtypeStruct((80, 128), BF16), i...  67.2 us

profile of v5, /device:TPU:2, one launch (start us, length us, event | category | flops | bytes accessed | tf_op | source)
XLA Modules:
  0.0 68.6 jit_solution(9211637724400900768)
XLA Ops:
  0.0 67.2 %shard_map.82 = bf16[80,128]{1,0:T(8,128)(2,1)} custom-call(bf16[256,576]{1,0:T(8,128)(2,1)} %bitcast.7, bf16[576,256]{1,0:T(8,128)(2,1)} %bitcast.8, bf16[512,576]{1,0:T(8,128)(2,1)} %bitcast.5, bf16[32,512,128]{2,1,0:T(8,128)(2,1)} %uv_hbm.1, bf16[80,4096]{1,0:T(8,128)(2,1)} %bitcast.6, s32[8]{0:T(128)} %len_ref.1, s32[64]{0:T(128)} %blocks_ref.1, s32[8]{0:T(128)} %reach_ref.1), custom_call_target="tpu_custom_call" | custom-call | tf_op jit(solution)/shard_map/pallas_call | solution.py:430
  67.2 1.3 %copy.10 = bf16[128,80]{0,1:T(8,128)(2,1)} copy(bf16[128,80]{0,1:T(8,128)(2,1)} %bitcast.9) | data formatting | bytes 40960

commit v6 on v5

--- a/solution.py
+++ b/solution.py
@@ -76,9 +76,6 @@
         sent.append(copy)
         return copy
 
-    m_ref[...] = jnp.full_like(m_ref, NEG)
-    l_ref[...] = jnp.zeros_like(l_ref)
-    acc[...] = jnp.zeros_like(acc)
     lanes = lax.broadcasted_iota(jnp.int32, (1, 64), 1)
     local[1].wait()
     own = (lanes == blocks_ref[b]).astype(F32)
@@ -135,6 +132,10 @@
     )
     qp.append(q_send(2, 0, 1, 1, yp))
     qm.append(q_send(3, 0, 3, 0, ym))
+
+    m_ref[...] = jnp.full_like(m_ref, NEG)
+    l_ref[...] = jnp.zeros_like(l_ref)
+    acc[...] = jnp.zeros_like(acc)
 
     local[2].wait()
 
@@ -349,6 +350,29 @@
         cross(0, half)
     place_unit(0, 0, 0)
     place_unit(0, 0, 1)
+    def sums(n, d, dh, who):
+        return pltpu.make_async_remote_copy(
+            src_ref=out_send.at[dh, 80 * d : 80 * d + 80], dst_ref=rs.at[n],
+            send_sem=rs_s.at[n], recv_sem=rs_r.at[n], device_id=who, device_id_type=MESH,
+        )
+
+    def project(to_p):
+        dp = (p + to_p) % 2
+        for dc in (1, 0):
+            to_c = c if dc == 0 else 1 - c
+            dh = 2 * dp + dc
+            rows = pl.ds(pl.multiple_of(128 * (2 * to_p + to_c), 128), 128)
+            out_send[dh] = dot(wbuf[...], hv_all[rows, :].astype(BF16), NT).astype(BF16)
+            for d in (2, 1, 3):
+                sums(4 * d + dh, d, dh, dev(y_=(y + 4 - d) % 4, p_=to_p, c_=to_c)).start()
+            if dc:
+                sums(dh, 0, dh, dev(p_=to_p, c_=to_c)).start()
+            else:
+
+                @pl.when(dp == 1)
+                def _():
+                    sums(2, 0, 2, dev(p_=1 - p)).start()
+
     done = 0
     while done < len(sent) and sent[done] is not hz[2, 0]:
         sent[done].wait_send()
@@ -389,30 +413,21 @@
     for r, half in ((3, 0), (5, 0), (3, 1), (5, 1)):
         hz[r, half].wait_recv()
         place_unit(r, 0, half)
+    for copy in ws:
+        copy.wait_recv()
+    project(xh)
     for r, half in (
         (1, 0), (7, 0), (1, 1), (7, 1), (3, 0), (5, 0), (4, 0), (3, 1), (5, 1), (4, 1)
     ):
         hx[r, half].wait_recv()
         place_unit(r, 1, half)
 
-    for copy in ws:
-        copy.wait_recv()
-    back = []
-    for dh in (3, 2, 1, 0):
-        h = peer(0, dh)[0]
-        rows = pl.ds(pl.multiple_of(128 * h, 128), 128)
-        out_send[dh] = dot(wbuf[...], hv_all[rows, :].astype(BF16), NT).astype(BF16)
-        for d in (2, 1, 3, 0):
-            if d or dh:
-                n = 4 * d + dh
-                back.append(
-                    send(
-                        out_send.at[dh, 80 * d : 80 * d + 80], rs.at[n],
-                        rs_s.at[n], rs_r.at[n], peer(d, dh),
-                    )
-                )
+    project(1 - xh)
     result = out_send[0, 0:80, :].astype(F32)
-    for copy in sent[done : len(sent) - len(back)]:
+    back = [
+        sums(4 * d + dh, d, dh, peer(d, dh)) for d in range(4) for dh in range(4) if d or dh
+    ]
+    for copy in sent[done:]:
         copy.wait_send()
     for copy in back:
         copy.wait_recv()

time: 69.5 us -> 68.3 us (0.983); the launches traced: 68.6 us -> 68.2 us
  no operation moved by 1% of the time
where the time goes in v6:
time: 68.3 us; the launch traced here: 68.2 us
  Pallas kernels  66.8 us (98%)
  local copies, waits for them, and re-layouts  1.34 us (2%)
    pallas_call x1, Pallas kernels, per_device(): pl.pallas_call(kernel, out_shape=jax.ShapeDtypeStruct((80, 128), BF16), i...  66.8 us

profile of v6, /device:TPU:2, one launch (start us, length us, event | category | flops | bytes accessed | tf_op | source)
XLA Modules:
  0.0 68.2 jit_solution(16339062349588624351)
XLA Ops:
  0.0 66.8 %shard_map.82 = bf16[80,128]{1,0:T(8,128)(2,1)} custom-call(bf16[256,576]{1,0:T(8,128)(2,1)} %bitcast.7, bf16[576,256]{1,0:T(8,128)(2,1)} %bitcast.8, bf16[512,576]{1,0:T(8,128)(2,1)} %bitcast.5, bf16[32,512,128]{2,1,0:T(8,128)(2,1)} %uv_hbm.1, bf16[80,4096]{1,0:T(8,128)(2,1)} %bitcast.6, s32[8]{0:T(128)} %len_ref.1, s32[64]{0:T(128)} %blocks_ref.1, s32[8]{0:T(128)} %reach_ref.1), custom_call_target="tpu_custom_call" | custom-call | tf_op jit(solution)/shard_map/pallas_call | solution.py:445
  66.8 1.3 %copy.10 = bf16[128,80]{0,1:T(8,128)(2,1)} copy(bf16[128,80]{0,1:T(8,128)(2,1)} %bitcast.9) | data formatting | bytes 40960
